TPU v7x, 32 devices: a whole 2x2x4 slice. The times are simulated.
32 devices in a mesh: grp: 2 (over y), run: 4 (over x, core), chan: 4 (over z).
Axes of the slice: x: 2, y: 2, z: 4, core: 2. Of those that a mesh axis runs over, the one named last changes fastest.
Arguments:
- embed: bfloat16 [512, 8192], P('grp', 'chan'), parts along dimension 0, may hold values from -6 to 6
- noise: bfloat16 [16, 32, 8192], P(('grp', 'run'), None, 'chan'), parts along dimension 0, may hold values from -12 to 12
- positions: int32 [16, 32], P(('grp', 'run')), parts along dimension 0, may hold values from 0 to 255
- restore: int32 [16, 2], P(('grp', 'run')), parts along dimension 0, may hold values 0 or 1
- short_one: float32 [7, 8192], P(None, 'chan'), may hold values from -2 to 2
- long_one: float32 [128, 8192], P(None, 'chan'), may hold values from -0.5 to 0.5
- out_weight: bfloat16 [8192, 8192], P(None, 'chan'), may hold values from -0.0625 to 0.0625
- short_two: float32 [7, 8192], P(None, 'chan'), may hold values from -2 to 2
- long_two: float32 [128, 8192], P(None, 'chan'), may hold values from -0.5 to 0.5
Outputs:
- traced: bfloat16 [16, 256, 8192], P(('grp', 'run'), None, 'chan'), parts along dimension 0
There are 2 independent parts, one for each index of `grp`. A program takes and returns all parts, laid end to end along the dimension named above; an argument that names none is the same for every part. Nothing has to cross between parts.
All inputs are finite; a program needn't handle non-finite values. No bound on the sum of `restore` on one device may be relied on, other than what follows from the above.
Results may differ from a plain program's by a relative error of at most 0.007.
Values may be sent and summed in bfloat16 or wider, within the bound.
A program may use at most 128 MiB of HBM per device.

v0:
```python
import jax
import jax.numpy as jnp
from jax import lax
from jax.sharding import PartitionSpec as P


def short_filter(field, filter_taps):
    length = field.shape[1]
    running = jnp.zeros(field.shape, jnp.float32)
    for shift_count in range(filter_taps.shape[0]):
        shifted = jnp.pad(field, ((0, 0), (shift_count, 0), (0, 0)))[:, :length]
        running = running + filter_taps[shift_count][None, None, :] * shifted
    return running


def block_filter(field, filter_taps):
    width = field.shape[2]
    span = filter_taps.shape[0]
    kernel = filter_taps[::-1][:, None, :]
    return lax.conv_general_dilated(
        field,
        kernel,
        window_strides=(1,),
        padding=((span - 1, 0),),
        dimension_numbers=("NWC", "WIO", "NWC"),
        feature_group_count=width,
        precision=lax.Precision.HIGHEST,
        preferred_element_type=jnp.float32,
    )


def per_device(
    embed, noise, positions, restore, short_one, long_one, out_weight, short_two, long_two
):
    run_count = noise.shape[0]
    length = embed.shape[0]
    first_run = lax.axis_index("run") * run_count
    run_ids = first_run + jnp.arange(run_count, dtype=jnp.int32)
    onehot = (jnp.arange(length, dtype=jnp.int32)[None, :, None] == positions[:, None, :]).astype(
        jnp.bfloat16
    )
    added = jnp.einsum("rlp,rpc->rlc", onehot, noise, preferred_element_type=jnp.float32)
    corrupt_flag = (run_ids != 0).astype(jnp.float32)[:, None, None]
    inputs = (embed.astype(jnp.float32)[None] + corrupt_flag * added).astype(jnp.bfloat16)
    batch_inputs = jnp.concatenate([inputs, embed[None]], axis=0)
    input_values = batch_inputs.astype(jnp.float32)
    filtered = block_filter(short_filter(input_values, short_one), long_one)
    mixed = (filtered * jax.nn.silu(input_values)).astype(jnp.bfloat16)
    initial = jnp.zeros((mixed.shape[0], length, out_weight.shape[1]), jnp.float32)
    segment = lax.all_gather(mixed, "chan", axis=2, tiled=True)
    weight_rows = lax.slice_in_dim(out_weight, 0, segment.shape[2], axis=0)
    projected = initial + jnp.einsum(
        "rlk,kc->rlc", segment, weight_rows, preferred_element_type=jnp.float32
    )
    hidden = (input_values + projected).astype(jnp.bfloat16)
    clean_hidden = hidden[run_count]
    hidden = hidden[:run_count]
    block_size = length // restore.shape[1]
    restored_rows = jnp.repeat(restore, block_size, axis=1)[:, :, None] == 1
    restored = jnp.where(restored_rows, clean_hidden[None], hidden)
    restored_values = restored.astype(jnp.float32)
    second = block_filter(short_filter(restored_values, short_two), long_two)
    return (restored_values + second * jax.nn.silu(restored_values)).astype(jnp.bfloat16)


def solution(mesh):
    in_specs = (
        P("grp", "chan"),
        P(("grp", "run"), None, "chan"),
        P(("grp", "run"), None),
        P(("grp", "run"), None),
        P(None, "chan"),
        P(None, "chan"),
        P(None, "chan"),
        P(None, "chan"),
        P(None, "chan"),
    )
    out_specs = P(("grp", "run"), None, "chan")
    return jax.shard_map(
        per_device, mesh=mesh, in_specs=in_specs, out_specs=out_specs, check_vma=False
    )
```

profile of v0, /device:TPU:0, one launch (start us, length us, event | category | flops | bytes accessed | tf_op | source)
XLA Modules:
  0.0 446.8 jit_solution(15623138889471099007)
XLA Ops:
  6.5 0.0 copy-start
  6.5 0.0 copy-start.6
  6.5 0.0 all-gather.2.cloned.1.call-start
  6.5 1.2 fusion.40
  7.8 0.0 copy-start.2
  7.8 2.9 convert_element_type.53
  10.7 8.9 %rev.6 = f32[128,2048]{1,0:T(8,128)} reverse(f32[128,2048]{1,0:T(8,128)} %param.14), dimensions={0} | reverse | bytes 2097152 | tf_op jit(solution)/shard_map/rev | solution.py:19
  19.5 0.0 copy-done
  19.5 0.0 copy-done.6
  19.5 2.4 add_convert_fusion.1
  22.0 0.0 copy-done.2
  22.0 0.4 maximum_convert_fusion
  22.4 0.0 copy-start.4
  22.4 5.2 %fusion.10 = f32[3,256,2048]{2,1,0:T(8,128)S(1)} fusion(f32[3,256,2048]{2,1,0:T(8,128)S(1)} %maximum_convert_fusion, f32[2048]{0:T(1024)S(1)} %bitcast.48, f32[2048]{0:T(1024)S(1)} %bitcast.49, f32[2048]{0:T(1024)S(1)} %bitcast.44, f32[2048]{0:T(1024)S(1)} %bitcast.45, f32[2048]{0:T(1024)S(1)} %bitcast.46, f32[2048]{0:T(1024)S(1)} %bitcast.47, ...), kind=kLoop, calls=%fused_computation.16 | loop fusion | flops 20447232 | bytes 12640256 | tf_op jit(solution)/shard_map/add | solution.py:12
  27.6 0.0 copy-done.4
  27.6 98.9 %fusion.2 = f32[3,256,2048]{2,0,1:T(4,128)S(1)} fusion(f32[3,256,2048]{2,1,0:T(8,128)S(1)} %fusion.10, f32[128,1,2048]{2,0,1:T(8,128)S(1)} %bitcast.35), kind=kOutput, calls=%fused_computation.2 | convolution fusion | flops 1816657920 | bytes 13631488 | tf_op jit(solution)/shard_map/conv_general_dilated | solution.py:20
  126.5 0.0 copy-start.7
  126.5 5.2 %fusion.16 = bf16[3,256,2048]{2,1,0:T(8,128)(2,1)} fusion(f32[3,256,2048]{2,0,1:T(4,128)S(1)} %fusion.2, bf16[1,256,2048]{2,1,0:T(8,128)(2,1)S(1)} %bitcast.32, bf16[2,256,2048]{2,1,0:T(8,128)(2,1)S(1)} %add_convert_fusion.1), kind=kLoop, calls=%fused_computation.23 | loop fusion | flops 12582912 | bytes 12582912 | tf_op jit(solution)/shard_map/convert_element_type | solution.py:48
  131.7 0.0 copy-start.5
  131.7 0.0 all-gather.2.cloned.1.call-update
  131.8 0.0 copy-done.7
  131.8 0.1 broadcast_bitcast_fusion
  131.9 8.9 %rev.7 = f32[128,2048]{1,0:T(8,128)} reverse(f32[128,2048]{1,0:T(8,128)} %param.17), dimensions={0} | reverse | bytes 2097152 | tf_op jit(solution)/shard_map/rev | solution.py:19
  140.7 0.0 copy-done.5
  140.8 212.0 %all-gather.2.cloned.1.call-done = bf16[3,256,8192]{2,1,0:T(8,128)(2,1)} async-done(((bf16[3,256,2048]{2,1,0:T(8,128)(2,1)}), bf16[3,256,8192]{2,1,0:T(8,128)(2,1)}) %all-gather.2.cloned.1.call-update) | async-done | bytes 12582928 | tf_op jit(solution)/shard_map/all_gather | solution.py:50
  352.8 33.6 %add_convert_fusion = bf16[3,256,2048]{2,1,0:T(8,128)(2,1)S(1)} fusion(bf16[3,256,8192]{2,1,0:T(8,128)(2,1)} %all-gather.2.cloned.1.call-done, bf16[8192,2048]{1,0:T(8,128)(2,1)} %param.15, bf16[1,256,2048]{2,1,0:T(8,128)(2,1)S(1)} %bitcast.33, bf16[2,256,2048]{2,1,0:T(8,128)(2,1)S(1)} %add_convert_fusion.1), kind=kOutput, calls=%fused_computation.24 | convolution fusion | flops 25776095232 | bytes 52428800 | tf_op jit(solution)/shard_map/rlk,kc->rlc/dot_general | solution.py:52
  386.5 0.1 slice_bitcast_fusion
  386.6 0.4 fusion.35
  386.9 0.0 copy-start.3
  386.9 3.5 fusion.23
  390.4 0.0 copy-done.3
  390.4 0.0 copy-start.1
  390.4 45.4 %fusion.31 = f32[2,256,2048]{2,0,1:T(2,128)S(1)} fusion(f32[2,256,2048]{2,1,0:T(8,128)S(1)} %fusion.23, f32[128,1,2048]{2,0,1:T(8,128)S(1)} %bitcast.34), kind=kOutput, calls=%fused_computation.46 | convolution fusion | flops 1211105280 | bytes 9437184 | tf_op jit(solution)/shard_map/conv_general_dilated | solution.py:20
  435.9 4.1 fusion.30
  439.9 0.0 copy-done.1
  (4 shorter events, 0.1 us)
Async XLA Ops:
  6.5 13.0 %copy-start = (bf16[2,32,2048]{2,1,0:T(8,128)(2,1)S(1)}, bf16[2,32,2048]{2,1,0:T(8,128)(2,1)}, u32[]{:S(2)}) copy-start(bf16[2,32,2048]{2,1,0:T(8,128)(2,1)} %param.10) | copy-start | bytes 786436
  6.5 13.0 %copy-start.6 = (s32[2,32]{1,0:T(2,128)S(1)}, s32[2,32]{1,0:T(2,128)}, u32[]{:S(2)}) copy-start(s32[2,32]{1,0:T(2,128)} %param.11) | copy-start | bytes 772
  6.5 346.3 %all-gather.2.cloned.1.call-start = ((), (), s32[]{:S(2)}) async-start(), calls=%async_computation | async-start | bytes 15728640 | tf_op jit(solution)/shard_map/all_gather | solution.py:50
  7.8 14.2 %copy-start.2 = (bf16[256,2048]{1,0:T(8,128)(2,1)S(1)}, bf16[256,2048]{1,0:T(8,128)(2,1)}, u32[]{:S(2)}) copy-start(bf16[256,2048]{1,0:T(8,128)(2,1)} %param.9) | copy-start | bytes 3145732
  22.4 5.2 %copy-start.4 = (f32[128,2048]{1,0:T(8,128)S(1)}, f32[128,2048]{1,0:T(8,128)}, u32[]{:S(2)}) copy-start(f32[128,2048]{1,0:T(8,128)} %rev.6) | copy-start | bytes 3145732
  126.5 5.3 %copy-start.7 = (s32[2,2]{1,0:T(2,128)S(1)}, s32[2,2]{1,0:T(2,128)}, u32[]{:S(2)}) copy-start(s32[2,2]{1,0:T(2,128)} %param.12) | copy-start | bytes 52
  131.7 9.0 %copy-start.5 = (f32[7,2048]{1,0:T(8,128)S(1)}, f32[7,2048]{1,0:T(8,128)}, u32[]{:S(2)}) copy-start(f32[7,2048]{1,0:T(8,128)} %param.16) | copy-start | bytes 172036
  386.9 3.5 copy-start.3
  390.4 49.5 %copy-start.1 = (bf16[2,32,2048]{2,1,0:T(8,128)(2,1)S(1)}, bf16[2,32,2048]{2,1,0:T(8,128)(2,1)}, u32[]{:S(2)}) copy-start(bf16[2,32,2048]{2,1,0:T(8,128)(2,1)} %param.10) | copy-start | bytes 786436
Sparse Core Ops, SparseCore 0:
  131.9 220.8 all-gather.1
where the time goes:
time: 448 us; the launch traced here: 447 us
  waiting for transfers between devices  212 us (47%)
  matrix products  180 us (40%)
  other arithmetic  21.6 us (5%)
  local copies, waits for them, and re-layouts  19.2 us (4%)
  between operations  13.6 us (3%)
    all_gather x1, waiting for transfers between devices, per_device(): segment = lax.all_gather(mixed, 'chan', axis=2, tiled=True)  212 us
    conv_general_dilated x2, matrix products, block_filter(): lax.conv_general_dilated(field, kernel, window_strides=(1,), padding=((sp...  144 us
    dot_general x1, matrix products, per_device(): jnp.einsum('rlk,kc->rlc', segment, weight_rows, preferred_element_type=jn...  33.6 us
    rev x2, local copies, waits for them, and re-layouts, block_filter(): kernel = filter_taps[::-1][:, None, :]  17.7 us
  transfers between devices with their start and end apart: 1, of which 1 were waited for; matrix products, arithmetic and copies ran while one was open for 2% of the time, Pallas kernels for 0%

commit v1 on v0

v1 whole, which is shorter than its diff:
```python
import functools

import jax
import jax.numpy as jnp
import numpy as np
from jax import lax
from jax.experimental import pallas as pl
from jax.experimental.pallas import tpu as pltpu
from jax.sharding import PartitionSpec as P


def transform_tables(length, taps_rows, size):
    half = size // 2
    angle = 2.0 * np.pi * (np.arange(half)[:, None] + 0.5) / size
    field = angle * np.arange(length)[None, :]
    taps = angle * np.arange(taps_rows)[None, :]
    forward = np.concatenate([np.cos(field), -np.sin(field)], axis=0)
    taps_forward = np.concatenate([np.cos(taps), -np.sin(taps)], axis=0)
    inverse = np.concatenate([np.cos(field), -np.sin(field)], axis=0).T * (2.0 / size)
    kinds = [jnp.asarray(table, dtype=jnp.bfloat16) for table in (forward, taps_forward, inverse)]
    return kinds


def dot(left, right):
    return jnp.dot(left, right, preferred_element_type=jnp.float32)


def gate(values):
    return 0.5 * values * (1.0 + jnp.tanh(0.5 * values))


def spectral_filter(field, spectrum_re, spectrum_im, forward, inverse):
    half = spectrum_re.shape[0]
    field_spectrum = dot(forward, field)
    re, im = field_spectrum[:half], field_spectrum[half:]
    out_re = (re * spectrum_re - im * spectrum_im).astype(jnp.bfloat16)
    out_im = (re * spectrum_im + im * spectrum_re).astype(jnp.bfloat16)
    return dot(inverse[:, :half], out_re) + dot(inverse[:, half:], out_im)


def project_kernel(
    embed, noise, onehot, taps, weight, forward, taps_forward, inverse, out
):
    step = pl.program_id(0)
    runs = noise.shape[1]
    length = embed.shape[1]
    half = forward.shape[0] // 2
    spectrum = dot(taps_forward[...], taps[0])
    spectrum_re, spectrum_im = spectrum[:half], spectrum[half:]

    @pl.when(step == 0)
    def _():
        out[...] = jnp.zeros_like(out)

    base = embed[0]
    for r in range(runs + 1):
        if r < runs:
            added = dot(onehot[r], noise[0, r])
            field = (base.astype(jnp.float32) + added).astype(jnp.bfloat16)
        else:
            field = base
        filtered = spectral_filter(
            field, spectrum_re, spectrum_im, forward[...], inverse[...]
        )
        mixed = (filtered * gate(field.astype(jnp.float32))).astype(jnp.bfloat16)
        rows = pl.ds(r * length, length)
        out[rows] += dot(mixed, weight[...])


def second_kernel(
    embed, noise, onehot, restore, taps, projected, forward, taps_forward, inverse, out
):
    runs = noise.shape[0]
    length = embed.shape[0]
    half = forward.shape[0] // 2
    spectrum = dot(taps_forward[...], taps[...])
    spectrum_re, spectrum_im = spectrum[:half], spectrum[half:]
    base = embed[...].astype(jnp.float32)
    clean = (base + projected[pl.ds(runs * length, length)]).astype(jnp.bfloat16)
    for r in range(runs):
        added = dot(onehot[r], noise[r])
        field = (base + added).astype(jnp.bfloat16).astype(jnp.float32)
        hidden = (field + projected[pl.ds(r * length, length)]).astype(jnp.bfloat16)
        flags = restore[r]
        values = jnp.where(flags == 1, clean.astype(jnp.float32), hidden.astype(jnp.float32))
        second = spectral_filter(
            values.astype(jnp.bfloat16), spectrum_re, spectrum_im, forward[...], inverse[...]
        )
        out[r] = (values + second * gate(values)).astype(jnp.bfloat16)


def combined_taps(short_taps, long_taps, rows):
    total = jnp.zeros((rows, long_taps.shape[1]), jnp.float32)
    for k in range(short_taps.shape[0]):
        shifted = jnp.pad(long_taps, ((k, rows - k - long_taps.shape[0]), (0, 0)))
        total = total + short_taps[k][None, :] * shifted
    return total.astype(jnp.bfloat16)


def whole(shape):
    return pl.BlockSpec(shape, lambda *_: (0,) * len(shape))


def per_device(
    embed, noise, positions, restore, short_one, long_one, out_weight, short_two, long_two
):
    runs, corrupted, width = noise.shape
    length = embed.shape[0]
    chan_count = lax.axis_size("chan")
    run_devices = lax.axis_size("run")
    run_index = lax.axis_index("run")
    run_ids = run_index * runs + jnp.arange(runs, dtype=jnp.int32)
    span = short_one.shape[0] + long_one.shape[0] - 1
    unit = 8 * run_devices
    taps_rows = -(-span // unit) * unit
    size = 512
    assert length + span - 1 <= size
    forward, taps_forward, inverse = transform_tables(length, taps_rows, size)

    onehot = (
        (jnp.arange(length, dtype=jnp.int32)[None, :, None] == positions[:, None, :])
        & (run_ids != 0)[:, None, None]
    ).astype(jnp.bfloat16)
    block_size = length // restore.shape[1]
    flags = jnp.repeat(restore, block_size, axis=1)[:, :, None]

    taps_one = combined_taps(short_one, long_one, taps_rows)
    taps_two = combined_taps(short_two, long_two, taps_rows)

    piece = jnp.concatenate(
        [
            lax.dynamic_slice_in_dim(
                embed, run_index * (length // run_devices), length // run_devices, axis=0
            ),
            lax.dynamic_slice_in_dim(
                taps_one, run_index * (taps_rows // run_devices), taps_rows // run_devices, axis=0
            ),
        ],
        axis=0,
    )
    shared = lax.all_gather(piece, ("chan", "run"), axis=0)
    rows_here = length // run_devices
    all_embed = shared[:, :rows_here].reshape(chan_count, length, width)
    all_taps = shared[:, rows_here:].reshape(chan_count, taps_rows, width)
    all_noise = lax.all_gather(noise, "chan", axis=0)

    tile = min(512, width)
    per = width // tile
    tables = [forward, taps_forward, inverse]
    table_specs = [whole(table.shape) for table in tables]
    projected = pl.pallas_call(
        project_kernel,
        grid=(chan_count * per,),
        in_specs=[
            pl.BlockSpec((1, length, tile), lambda i: (i // per, 0, i % per)),
            pl.BlockSpec((1, runs, corrupted, tile), lambda i: (i // per, 0, 0, i % per)),
            whole(onehot.shape),
            pl.BlockSpec((1, taps_rows, tile), lambda i: (i // per, 0, i % per)),
            pl.BlockSpec((tile, width), lambda i: (i, 0)),
            *table_specs,
        ],
        out_specs=whole(((runs + 1) * length, width)),
        out_shape=jax.ShapeDtypeStruct(((runs + 1) * length, width), jnp.float32),
        compiler_params=pltpu.CompilerParams(vmem_limit_bytes=56 * 2**20),
    )(all_embed, all_noise, onehot, all_taps, out_weight, *tables)

    tile = min(256, width)
    return pl.pallas_call(
        second_kernel,
        grid=(width // tile,),
        in_specs=[
            pl.BlockSpec((length, tile), lambda i: (0, i)),
            pl.BlockSpec((runs, corrupted, tile), lambda i: (0, 0, i)),
            whole(onehot.shape),
            whole(flags.shape),
            pl.BlockSpec((taps_rows, tile), lambda i: (0, i)),
            pl.BlockSpec(((runs + 1) * length, tile), lambda i: (0, i)),
            *table_specs,
        ],
        out_specs=pl.BlockSpec((runs, length, tile), lambda i: (0, 0, i)),
        out_shape=jax.ShapeDtypeStruct((runs, length, width), jnp.bfloat16),
        compiler_params=pltpu.CompilerParams(vmem_limit_bytes=56 * 2**20),
    )(embed, noise, onehot, flags, taps_two, projected, *tables)


def solution(mesh):
    in_specs = (
        P("grp", "chan"),
        P(("grp", "run"), None, "chan"),
        P(("grp", "run"), None),
        P(("grp", "run"), None),
        P(None, "chan"),
        P(None, "chan"),
        P(None, "chan"),
        P(None, "chan"),
        P(None, "chan"),
    )
    out_specs = P(("grp", "run"), None, "chan")
    return jax.shard_map(
        per_device, mesh=mesh, in_specs=in_specs, out_specs=out_specs, check_vma=False
    )
```

time: 448 us -> 199 us (0.44)
  matrix products: 180 us -> 0 us
  waiting for transfers between devices: 212 us -> 83.7 us
  Pallas kernels: 0 us -> 83.5 us
  other arithmetic: 21.6 us -> 6.23 us
  local copies, waits for them, and re-layouts: 19.2 us -> 11.8 us
    conv_general_dilated x2 -> x0, matrix products: 144 us -> none  [block_filter(): lax.conv_general_dilated(field, kernel, window_strides=(1,), padding=((sp...]
    all_gather x1 -> x2, waiting for transfers between devices: 212 us -> 83 us  [the longest x1 63.4 us: per_device(): shared = lax.all_gather(piece, ('chan', 'run'), axis=0)]
    pallas_call x0 -> x2, Pallas kernels: none -> 83.5 us  [the longest x1 71 us: per_device(): pl.pallas_call(project_kernel, grid=(chan_count * per,), in_specs=[pl.Blo...]
    dot_general x2 -> x0, matrix products: 36.1 us -> none  [the longest x1 33.6 us: per_device(): jnp.einsum('rlk,kc->rlc', segment, weight_rows, preferred_element_type=jn...]
    rev x2 -> x0, local copies, waits for them, and re-layouts: 17.7 us -> none  [block_filter(): kernel = filter_taps[::-1][:, None, :]]
    convert_element_type x6 -> x3, other arithmetic: 12.9 us -> 2.85 us  [the longest x2 2.11 us: combined_taps(): return total.astype(jnp.bfloat16)]
    slice x2 -> x4, local copies, waits for them, and re-layouts: 1.26 us -> 9.8 us  [the longest x1 4.84 us: per_device(): all_embed = shared[:, :rows_here].reshape(chan_count, length, width)]
    add x2 -> x1, other arithmetic: 8.62 us -> 2.58 us  [combined_taps(): total = total + short_taps[k][None, :] * shifted]
  transfers between devices with their start and end apart: 1 -> 2, of which waited for: 1 -> 2; matrix products, arithmetic and copies ran while one was open for 2% -> 6% of each run, Pallas kernels for 0% -> 0%
where the time goes in v1:
time: 199 us
  waiting for transfers between devices  83.7 us (42%)
  Pallas kernels  83.5 us (42%)
  between operations  13.5 us (7%)
  local copies, waits for them, and re-layouts  11.8 us (6%)
  other arithmetic  6.23 us (3%)
    pallas_call x1, Pallas kernels, per_device(): pl.pallas_call(project_kernel, grid=(chan_count * per,), in_specs=[pl.Blo...  71 us
    all_gather x1, waiting for transfers between devices, per_device(): shared = lax.all_gather(piece, ('chan', 'run'), axis=0)  63.4 us
    all_gather x1, waiting for transfers between devices, per_device(): all_noise = lax.all_gather(noise, 'chan', axis=0)  19.5 us
    pallas_call x1, Pallas kernels, per_device(): pl.pallas_call(second_kernel, grid=(width // tile,), in_specs=[pl.BlockSp...  12.4 us
    slice x1, local copies, waits for them, and re-layouts, per_device(): all_embed = shared[:, :rows_here].reshape(chan_count, length, width)  4.84 us
  transfers between devices with their start and end apart: 2, of which 2 were waited for; matrix products, arithmetic and copies ran while one was open for 6% of the time, Pallas kernels for 0%

profile of v1, /device:TPU:0, one launch (start us, length us, event | category | flops | bytes accessed | tf_op | source)
XLA Modules:
  0.0 198.7 jit_solution(9975549344917766263)
XLA Ops:
  6.5 0.0 all-gather.5.cloned.1.call-start
  6.5 1.2 fusion.11
  7.8 1.0 constant_dynamic-slice_fusion
  8.7 0.0 copy-start
  8.8 2.6 %multiply_add_fusion = (f32[160,2048]{1,0:T(8,128)S(1)}, f32[160,2048]{1,0:T(8,128)S(1)}) fusion(f32[128,2048]{1,0:T(8,128)} %param.17, f32[2048]{0:T(1024)S(1)} %bitcast.35, f32[2048]{0:T(1024)S(1)} %bitcast.36, f32[2048]{0:T(1024)S(1)} %bitcast.34), kind=kLoop, calls=%fused_computation.5 | loop fusion | flops 1310720 | bytes 3694592 | tf_op jit(solution)/shard_map/add | solution.py:96
  11.3 0.0 copy-done
  11.4 0.0 copy-start.4
  11.4 0.3 fusion.5
  11.7 0.0 copy-start.3
  11.7 0.0 copy-start.2
  11.7 0.0 copy-start.1
  11.7 0.8 pad_maximum_fusion
  12.5 0.0 all-gather.5.cloned.1.call-update
  12.5 0.0 all-gather.7.cloned.1.call-start
  12.6 0.7 all-gather.7.cloned.1.call-update
  13.3 0.0 copy-done.4
  13.3 0.1 broadcast_in_dim.2
  13.4 0.9 broadcast_in_dim_reshape.4.restore
  14.3 0.0 copy-done.3
  14.3 0.7 fusion.10.onehot
  15.1 0.0 copy-done.2
  15.1 0.0 copy-done.1
  15.1 1.8 add_convert_fusion.taps
  16.9 63.4 %all-gather.5.cloned.1.call-done = bf16[1664,2048]{1,0:T(8,128)(2,1)} async-done(((bf16[104,2048]{1,0:T(8,128)(2,1)}), bf16[1664,2048]{1,0:T(8,128)(2,1)}) %all-gather.5.cloned.1.call-update) | async-done | bytes 6815760 | tf_op jit(solution)/shard_map/all_gather | solution.py:141
  80.4 4.8 %slice.64 = bf16[16,64,2048]{2,1,0:T(8,128)(2,1)} slice(bf16[16,104,2048]{2,1,0:T(8,128)(2,1)} %bitcast.20), slice={[0:16], [0:64], [0:2048]} | slice | bytes 8388608 | tf_op jit(solution)/shard_map/slice | solution.py:143
  85.2 3.7 %slice.65 = bf16[16,40,2048]{2,1,0:T(8,128)(2,1)} slice(bf16[16,104,2048]{2,1,0:T(8,128)(2,1)} %bitcast.21), slice={[0:16], [64:104], [0:2048]} | slice | bytes 5242880 | tf_op jit(solution)/shard_map/slice | solution.py:144
  88.9 19.5 %all-gather.7.cloned.1.call-done = bf16[8,32,2048]{2,1,0:T(8,128)(2,1)} async-done(((bf16[2,32,2048]{2,1,0:T(8,128)(2,1)}), bf16[8,32,2048]{2,1,0:T(8,128)(2,1)}) %all-gather.7.cloned.1.call-update) | async-done | bytes 1048592 | tf_op jit(solution)/shard_map/all_gather | solution.py:145
  108.4 71.0 %shard_map.118.projected = f32[768,2048]{1,0:T(8,128)} custom-call(bf16[4,256,2048]{2,1,0:T(8,128)(2,1)} %bitcast.18, bf16[4,2,32,2048]{3,2,1,0:T(8,128)(2,1)} %bitcast.22, bf16[2,256,32]{2,1,0:T(8,128)(2,1)} %fusion.10.onehot, bf16[4,160,2048]{2,1,0:T(8,128)(2,1)} %bitcast.19, bf16[8192,2048]{1,0:T(8,128)(2,1)} %weight.1, ...), custom_call_target="tpu_custom_call" | custom-call | tf_op jit(solution)/shard_map/pallas_call | solution.py:151
  179.4 12.4 %shard_map.119 = bf16[2,256,2048]{2,1,0:T(8,128)(2,1)} custom-call(bf16[256,2048]{1,0:T(8,128)(2,1)} %embed.1, bf16[2,32,2048]{2,1,0:T(8,128)(2,1)} %noise.1, bf16[2,256,32]{2,1,0:T(8,128)(2,1)} %fusion.10.onehot, s32[2,256,1]{2,1,0:T(8,128)} %broadcast_in_dim_reshape.4.restore, bf16[160,2048]{1,0:T(8,128)(2,1)} %add_convert_fusion.taps, ...), custom_call_target="tpu_custom_call" | custom-call | tf_op jit(solution)/shard_map/pallas_call | solution.py:168
  (2 shorter events, 0.0 us)
Async XLA Ops:
  6.5 73.8 %all-gather.5.cloned.1.call-start = ((), (), s32[]{:S(2)}) async-start(), calls=%async_computation | async-start | bytes 7241728 | tf_op jit(solution)/shard_map/all_gather | solution.py:141
  8.7 2.6 %copy-start = (f32[128,2048]{1,0:T(8,128)S(1)}, f32[128,2048]{1,0:T(8,128)}, u32[]{:S(2)}) copy-start(f32[128,2048]{1,0:T(8,128)} %param.17) | copy-start | bytes 3145732
  11.4 1.9 copy-start.4
  11.7 2.6 %copy-start.3 = (s32[2,32]{1,0:T(2,128)S(1)}, s32[2,32]{1,0:T(2,128)}, u32[]{:S(2)}) copy-start(s32[2,32]{1,0:T(2,128)} %param.14) | copy-start | bytes 772
  11.7 3.4 %copy-start.2 = (f32[7,2048]{1,0:T(8,128)S(1)}, f32[7,2048]{1,0:T(8,128)}, u32[]{:S(2)}) copy-start(f32[7,2048]{1,0:T(8,128)} %param.19) | copy-start | bytes 172036
  11.7 3.4 %copy-start.1 = (f32[128,2048]{1,0:T(8,128)S(1)}, f32[128,2048]{1,0:T(8,128)}, u32[]{:S(2)}) copy-start(f32[128,2048]{1,0:T(8,128)} %param.20) | copy-start | bytes 3145732
  12.5 95.9 %all-gather.7.cloned.1.call-start = ((), (), s32[]{:S(2)}) async-start(), calls=%async_computation.1 | async-start | bytes 1310720 | tf_op jit(solution)/shard_map/all_gather | solution.py:145
Sparse Core Ops, SparseCore 0:
  12.7 67.6 all-gather.4
  81.9 26.4 all-gather.6

commit v2 on v1

--- a/solution.py
+++ b/solution.py
@@ -38,24 +38,141 @@
     return dot(inverse[:, :half], out_re) + dot(inverse[:, half:], out_im)
 
 
+def exclusive_or(left, right, count):
+    total, bit = 0, 1
+    while bit < count:
+        total = total + bit * ((left // bit + right // bit) % 2)
+        bit *= 2
+    return total
+
+
 def project_kernel(
-    embed, noise, onehot, taps, weight, forward, taps_forward, inverse, out
+    chan_count, run_devices, per, length,
+    own_ref, noise_ref, onehot, weight, forward, taps_forward, inverse, out,
+    shared, noises, local_sem, z_send, z_recv, n_send, n_recv, x_send, x_recv, s_send, s_recv,
 ):
     step = pl.program_id(0)
-    runs = noise.shape[1]
-    length = embed.shape[1]
+    k = step // per
+    j = step % per
+    me = lax.axis_index("chan")
+    run = lax.axis_index("run")
+    row, core = run // 2, run % 2
+    rows_x = run_devices // 2
+    runs = onehot.shape[0]
+    corrupted = onehot.shape[2]
     half = forward.shape[0] // 2
-    spectrum = dot(taps_forward[...], taps[0])
+    rows_here = length // run_devices
+    tile = weight.shape[0]
+    mesh_ids = pl.DeviceIdType.MESH
+
+    def remote(source, target, send, recv, device):
+        return pltpu.make_async_remote_copy(
+            src_ref=source, dst_ref=target, send_sem=send, recv_sem=recv,
+            device_id=device, device_id_type=mesh_ids,
+        )
+
+    def to_chan(q):
+        peer = {"chan": exclusive_or(me, q, chan_count)}
+        slot = shared.at[me, run]
+        return (
+            remote(slot, slot, z_send.at[q], z_recv.at[q], peer),
+            remote(noises.at[me], noises.at[me], n_send.at[q], n_recv.at[q], peer),
+        )
+
+    def from_chan(q):
+        other = exclusive_or(me, q, chan_count)
+        peer = {"chan": other}
+        slot = shared.at[other, run]
+        return (
+            remote(slot, slot, z_send.at[q], z_recv.at[q], peer),
+            remote(noises.at[other], noises.at[other], n_send.at[q], n_recv.at[q], peer),
+        )
+
+    def to_row(q, m):
+        slot = shared.at[exclusive_or(me, q, chan_count), run]
+        peer = {"run": ((row + m) % rows_x) * 2 + core}
+        return remote(slot, slot, x_send.at[q, m], x_recv.at[q, m], peer)
+
+    def from_row(q, m):
+        source = ((row + rows_x - m) % rows_x) * 2 + core
+        slot = shared.at[exclusive_or(me, q, chan_count), source]
+        return remote(slot, slot, x_send.at[q, m], x_recv.at[q, m], {"run": source})
+
+    def to_core(q, m):
+        slot = shared.at[
+            exclusive_or(me, q, chan_count), ((row + rows_x - m) % rows_x) * 2 + core
+        ]
+        return remote(slot, slot, s_send.at[q, m], s_recv.at[q, m], {"run": row * 2 + 1 - core})
+
+    def from_core(q, m):
+        slot = shared.at[
+            exclusive_or(me, q, chan_count), ((row + rows_x - m) % rows_x) * 2 + 1 - core
+        ]
+        return remote(slot, slot, s_send.at[q, m], s_recv.at[q, m], {"run": row * 2 + 1 - core})
+
+    @pl.when(step == 0)
+    def _():
+        first = pltpu.make_async_copy(own_ref, shared.at[me], local_sem.at[0])
+        second = pltpu.make_async_copy(noise_ref, noises.at[me], local_sem.at[1])
+        first.start()
+        second.start()
+        barrier = pltpu.get_barrier_semaphore()
+        for q in range(1, chan_count):
+            pl.semaphore_signal(
+                barrier, inc=1, device_id={"chan": exclusive_or(me, q, chan_count)},
+                device_id_type=mesh_ids,
+            )
+        for m in range(1, rows_x):
+            pl.semaphore_signal(
+                barrier, inc=1, device_id={"run": ((row + m) % rows_x) * 2 + core},
+                device_id_type=mesh_ids,
+            )
+        pl.semaphore_signal(
+            barrier, inc=1, device_id={"run": row * 2 + 1 - core}, device_id_type=mesh_ids
+        )
+        pl.semaphore_wait(barrier, chan_count - 1 + rows_x)
+        first.wait()
+        second.wait()
+        out[...] = jnp.zeros_like(out)
+
+    for q in range(1, chan_count):
+        @pl.when(step == q - 1)
+        def _():
+            for copy in to_chan(q):
+                copy.start()
+
+    @pl.when((j == 0) & (k > 0))
+    def _():
+        for m in range(rows_x):
+            from_core(k, m).wait_recv()
+        from_chan(k)[1].wait_recv()
+
+    @pl.when((j == per - 2) & (k < chan_count - 1))
+    def _():
+        from_chan(k + 1)[0].wait_recv()
+        for m in range(1, rows_x):
+            to_row(k + 1, m).start()
+        to_core(k + 1, 0).start()
+
+    @pl.when((j == per - 1) & (k < chan_count - 1))
+    def _():
+        for m in range(1, rows_x):
+            from_row(k + 1, m).wait_recv()
+            to_core(k + 1, m).start()
+
+    source = exclusive_or(me, k, chan_count)
+    columns = pl.ds(pl.multiple_of(j * tile, tile), tile)
+    base = jnp.concatenate(
+        [shared[source, r, :rows_here, columns] for r in range(run_devices)], axis=0
+    )
+    taps = jnp.concatenate(
+        [shared[source, r, rows_here:, columns] for r in range(run_devices)], axis=0
+    )
+    spectrum = dot(taps_forward[...], taps)
     spectrum_re, spectrum_im = spectrum[:half], spectrum[half:]
-
-    @pl.when(step == 0)
-    def _():
-        out[...] = jnp.zeros_like(out)
-
-    base = embed[0]
     for r in range(runs + 1):
         if r < runs:
-            added = dot(onehot[r], noise[0, r])
+            added = dot(onehot[r], noises[source, r * corrupted:(r + 1) * corrupted, columns])
             field = (base.astype(jnp.float32) + added).astype(jnp.bfloat16)
         else:
             field = base
@@ -65,6 +182,16 @@
         mixed = (filtered * gate(field.astype(jnp.float32))).astype(jnp.bfloat16)
         rows = pl.ds(r * length, length)
         out[rows] += dot(mixed, weight[...])
+
+    @pl.when(step == chan_count * per - 1)
+    def _():
+        for q in range(1, chan_count):
+            for copy in to_chan(q):
+                copy.wait_send()
+            for m in range(1, rows_x):
+                to_row(q, m).wait_send()
+            for m in range(rows_x):
+                to_core(q, m).wait_send()
 
 
 def second_kernel(
@@ -111,7 +238,7 @@
     run_index = lax.axis_index("run")
     run_ids = run_index * runs + jnp.arange(runs, dtype=jnp.int32)
     span = short_one.shape[0] + long_one.shape[0] - 1
-    unit = 8 * run_devices
+    unit = 16 * run_devices
     taps_rows = -(-span // unit) * unit
     size = 512
     assert length + span - 1 <= size
@@ -127,42 +254,53 @@
     taps_one = combined_taps(short_one, long_one, taps_rows)
     taps_two = combined_taps(short_two, long_two, taps_rows)
 
-    piece = jnp.concatenate(
+    rows_here = length // run_devices
+    own = jnp.concatenate(
         [
-            lax.dynamic_slice_in_dim(
-                embed, run_index * (length // run_devices), length // run_devices, axis=0
-            ),
-            lax.dynamic_slice_in_dim(
-                taps_one, run_index * (taps_rows // run_devices), taps_rows // run_devices, axis=0
-            ),
+            embed.reshape(run_devices, rows_here, width),
+            taps_one.reshape(run_devices, taps_rows // run_devices, width),
         ],
-        axis=0,
-    )
-    shared = lax.all_gather(piece, ("chan", "run"), axis=0)
-    rows_here = length // run_devices
-    all_embed = shared[:, :rows_here].reshape(chan_count, length, width)
-    all_taps = shared[:, rows_here:].reshape(chan_count, taps_rows, width)
-    all_noise = lax.all_gather(noise, "chan", axis=0)
-
-    tile = min(512, width)
-    per = width // tile
+        axis=1,
+    )
+    per = 4
+    tile = width // per
+    rows_x = run_devices // 2
     tables = [forward, taps_forward, inverse]
     table_specs = [whole(table.shape) for table in tables]
+    anywhere = pl.BlockSpec(memory_space=pl.ANY)
+
+    def weight_block(i):
+        return exclusive_or(lax.axis_index("chan"), i // per, chan_count) * per + i % per, 0
+
     projected = pl.pallas_call(
-        project_kernel,
+        functools.partial(project_kernel, chan_count, run_devices, per, length),
         grid=(chan_count * per,),
         in_specs=[
-            pl.BlockSpec((1, length, tile), lambda i: (i // per, 0, i % per)),
-            pl.BlockSpec((1, runs, corrupted, tile), lambda i: (i // per, 0, 0, i % per)),
+            anywhere,
+            anywhere,
             whole(onehot.shape),
-            pl.BlockSpec((1, taps_rows, tile), lambda i: (i // per, 0, i % per)),
-            pl.BlockSpec((tile, width), lambda i: (i, 0)),
+            pl.BlockSpec((tile, width), weight_block),
             *table_specs,
         ],
         out_specs=whole(((runs + 1) * length, width)),
         out_shape=jax.ShapeDtypeStruct(((runs + 1) * length, width), jnp.float32),
-        compiler_params=pltpu.CompilerParams(vmem_limit_bytes=56 * 2**20),
-    )(all_embed, all_noise, onehot, all_taps, out_weight, *tables)
+        scratch_shapes=[
+            pltpu.VMEM((chan_count, *own.shape), jnp.bfloat16),
+            pltpu.VMEM((chan_count, runs * corrupted, width), jnp.bfloat16),
+            pltpu.SemaphoreType.DMA((2,)),
+            pltpu.SemaphoreType.DMA((chan_count,)),
+            pltpu.SemaphoreType.DMA((chan_count,)),
+            pltpu.SemaphoreType.DMA((chan_count,)),
+            pltpu.SemaphoreType.DMA((chan_count,)),
+            pltpu.SemaphoreType.DMA((chan_count, rows_x)),
+            pltpu.SemaphoreType.DMA((chan_count, rows_x)),
+            pltpu.SemaphoreType.DMA((chan_count, rows_x)),
+            pltpu.SemaphoreType.DMA((chan_count, rows_x)),
+        ],
+        compiler_params=pltpu.CompilerParams(
+            vmem_limit_bytes=56 * 2**20, collective_id=0, has_side_effects=True
+        ),
+    )(own, noise.reshape(runs * corrupted, width), onehot, out_weight, *tables)
 
     tile = min(256, width)
     return pl.pallas_call(

time: 199 us -> 135 us (0.68)
  waiting for transfers between devices: 83.7 us -> 0 us
  Pallas kernels: 83.5 us -> 121 us
  between operations: 13.5 us -> 0.03 us
  local copies, waits for them, and re-layouts: 11.8 us -> 4.2 us
  other arithmetic: 6.23 us -> 9.56 us
    all_gather x2 -> x0, waiting for transfers between devices: 83 us -> none  [the longest x1 63.4 us: per_device(): shared = lax.all_gather(piece, ('chan', 'run'), axis=0)]
    pallas_call x1, Pallas kernels: 71 us -> 108 us  [per_device(): pl.pallas_call(functools.partial(project_kernel, chan_count, run_devices,...]
    slice x2 -> x0, local copies, waits for them, and re-layouts: 8.54 us -> none  [the longest x1 4.84 us: per_device(): all_embed = shared[:, :rows_here].reshape(chan_count, length, width)]
    convert_element_type x2, other arithmetic: 2.11 us -> 6.74 us  [combined_taps(): return total.astype(jnp.bfloat16)]
    add x1 -> x0, other arithmetic: 2.58 us -> none  [combined_taps(): total = total + short_taps[k][None, :] * shifted]
  transfers between devices with their start and end apart: 2 -> 0, of which waited for: 2 -> 0; matrix products, arithmetic and copies ran while one was open for 6% -> 0% of each run, Pallas kernels for 0% -> 0%
where the time goes in v2:
time: 135 us
  Pallas kernels  121 us (90%)
  other arithmetic  9.56 us (7%)
  local copies, waits for them, and re-layouts  4.2 us (3%)
    pallas_call x1, Pallas kernels, per_device(): pl.pallas_call(functools.partial(project_kernel, chan_count, run_devices,...  108 us
    pallas_call x1, Pallas kernels, per_device(): pl.pallas_call(second_kernel, grid=(width // tile,), in_specs=[pl.BlockSp...  12.5 us
    convert_element_type x2, other arithmetic, combined_taps(): return total.astype(jnp.bfloat16)  6.74 us

profile of v2, /device:TPU:0, one launch (start us, length us, event | category | flops | bytes accessed | tf_op | source)
XLA Modules:
  0.0 134.7 jit_solution(14620908403393107353)
XLA Ops:
  0.0 0.0 copy-start.1
  0.0 0.8 broadcast_in_dim.2
  0.8 1.2 fusion.2
  2.1 1.2 fusion.3
  3.3 1.4 %fusion.1.onehot = bf16[2,256,32]{2,1,0:T(8,128)(2,1)} fusion(s32[2,32]{1,0:T(2,128)} %param.14, pred[2]{0:T(512)(128)(4,1)S(1)} %add_compare_fusion), kind=kLoop, calls=%fused_computation.5 | loop fusion | flops 49152 | bytes 33026 | tf_op jit(solution)/shard_map/convert_element_type | solution.py:250
  4.7 0.9 broadcast_in_dim_reshape.4.restore
  5.6 0.0 copy-start
  5.6 5.8 %add_convert_fusion.1.taps = bf16[192,2048]{1,0:T(8,128)(2,1)} fusion(f32[128,2048]{1,0:T(8,128)} %param.20, f32[2048]{0:T(1024)S(1)} %bitcast.32, f32[2048]{0:T(1024)S(1)} %bitcast.33, f32[2048]{0:T(1024)S(1)} %bitcast.28, f32[2048]{0:T(1024)S(1)} %bitcast.29, f32[2048]{0:T(1024)S(1)} %bitcast.30, f32[2048]{0:T(1024)S(1)} %bitcast.31, f32[2048]{0:T(1024)S(1)} %bitcast.27), kind=kLoop, calls=%fused_computation.2 | loop fusion | flops 5505024 | bytes 1892352 | tf_op jit(solution)/shard_map/convert_element_type | solution.py:224
  11.4 0.0 copy-done.1
  11.4 0.9 add_convert_fusion
  12.4 0.0 copy-done
  12.4 1.4 %pad_maximum_fusion.own_ref = bf16[4,112,2048]{2,1,0:T(8,128)(2,1)} fusion(bf16[4,48,2048]{2,1,0:T(8,128)(2,1)S(1)} %bitcast.18, bf16[4,64,2048]{2,1,0:T(8,128)(2,1)S(1)} %bitcast.17), kind=kLoop, calls=%fused_computation | loop fusion | flops 3670016 | bytes 3670016 | tf_op jit(solution)/shard_map/concatenate | solution.py:258
  13.8 108.3 %shard_map.118.projected = f32[768,2048]{1,0:T(8,128)} custom-call(bf16[4,112,2048]{2,1,0:T(8,128)(2,1)} %pad_maximum_fusion.own_ref, bf16[64,2048]{1,0:T(8,128)(2,1)} %bitcast.19, bf16[2,256,32]{2,1,0:T(8,128)(2,1)} %fusion.1.onehot, bf16[8192,2048]{1,0:T(8,128)(2,1)} %weight.1, bf16[512,256]{1,0:T(8,128)(2,1)} %constant.18.clone.forward, ...), custom_call_target="tpu_custom_call" | custom-call | tf_op jit(solution)/shard_map/pallas_call | solution.py:275
  122.1 12.5 %shard_map.119 = bf16[2,256,2048]{2,1,0:T(8,128)(2,1)} custom-call(bf16[256,2048]{1,0:T(8,128)(2,1)} %embed.1, bf16[2,32,2048]{2,1,0:T(8,128)(2,1)} %noise.1, bf16[2,256,32]{2,1,0:T(8,128)(2,1)} %fusion.1.onehot, s32[2,256,1]{2,1,0:T(8,128)} %broadcast_in_dim_reshape.4.restore, bf16[192,2048]{1,0:T(8,128)(2,1)} %add_convert_fusion.1.taps, ...), custom_call_target="tpu_custom_call" | custom-call | tf_op jit(solution)/shard_map/pallas_call | solution.py:306
  (1 shorter events, 0.0 us)
Async XLA Ops:
  0.0 11.4 %copy-start.1 = (f32[128,2048]{1,0:T(8,128)S(1)}, f32[128,2048]{1,0:T(8,128)}, u32[]{:S(2)}) copy-start(f32[128,2048]{1,0:T(8,128)} %param.17) | copy-start | bytes 3145732
  5.6 6.8 %copy-start = (bf16[256,2048]{1,0:T(8,128)(2,1)S(1)}, bf16[256,2048]{1,0:T(8,128)(2,1)}, u32[]{:S(2)}) copy-start(bf16[256,2048]{1,0:T(8,128)(2,1)} %embed.1) | copy-start | bytes 3145732

commit v3 on v2

--- a/solution.py
+++ b/solution.py
@@ -79,6 +79,15 @@
             remote(noises.at[me], noises.at[me], n_send.at[q], n_recv.at[q], peer),
         )
 
+    def pass_on(q):
+        chunk = exclusive_or(me, q - 1, chan_count)
+        peer = {"chan": exclusive_or(me, 1, chan_count)}
+        slot = shared.at[chunk, run]
+        return (
+            remote(slot, slot, z_send.at[q], z_recv.at[q], peer),
+            remote(noises.at[chunk], noises.at[chunk], n_send.at[q], n_recv.at[q], peer),
+        )
+
     def from_chan(q):
         other = exclusive_or(me, q, chan_count)
         peer = {"chan": other}
@@ -135,7 +144,8 @@
         second.wait()
         out[...] = jnp.zeros_like(out)
 
-    for q in range(1, chan_count):
+    direct = [q for q in range(1, chan_count) if q == 1 or q % 2 == 0]
+    for q in direct:
         @pl.when(step == q - 1)
         def _():
             for copy in to_chan(q):
@@ -145,14 +155,19 @@
     def _():
         for m in range(rows_x):
             from_core(k, m).wait_recv()
-        from_chan(k)[1].wait_recv()
 
     @pl.when((j == per - 2) & (k < chan_count - 1))
     def _():
-        from_chan(k + 1)[0].wait_recv()
+        for copy in from_chan(k + 1):
+            copy.wait_recv()
         for m in range(1, rows_x):
             to_row(k + 1, m).start()
         to_core(k + 1, 0).start()
+
+    @pl.when((j == per - 2) & (k % 2 == 1) & (k < chan_count - 2))
+    def _():
+        for copy in pass_on(k + 2):
+            copy.start()
 
     @pl.when((j == per - 1) & (k < chan_count - 1))
     def _():
@@ -186,7 +201,7 @@
     @pl.when(step == chan_count * per - 1)
     def _():
         for q in range(1, chan_count):
-            for copy in to_chan(q):
+            for copy in to_chan(q) if q in direct else pass_on(q):
                 copy.wait_send()
             for m in range(1, rows_x):
                 to_row(q, m).wait_send()

time: 135 us -> 141 us (1.044)
  Pallas kernels: 121 us -> 127 us
    pallas_call x1, Pallas kernels: 108 us -> 114 us  [per_device(): pl.pallas_call(functools.partial(project_kernel, chan_count, run_devices,...]
where the time goes in v3:
time: 141 us
  Pallas kernels  127 us (90%)
  other arithmetic  9.56 us (7%)
  local copies, waits for them, and re-layouts  4.2 us (3%)
    pallas_call x1, Pallas kernels, per_device(): pl.pallas_call(functools.partial(project_kernel, chan_count, run_devices,...  114 us
    pallas_call x1, Pallas kernels, per_device(): pl.pallas_call(second_kernel, grid=(width // tile,), in_specs=[pl.BlockSp...  12.5 us
    convert_element_type x2, other arithmetic, combined_taps(): return total.astype(jnp.bfloat16)  6.74 us

profile of v3, /device:TPU:0, one launch (start us, length us, event | category | flops | bytes accessed | tf_op | source)
XLA Modules:
  0.0 140.8 jit_solution(1710886728862553329)
XLA Ops:
  0.0 0.0 copy-start.1
  0.0 0.8 broadcast_in_dim.2
  0.8 1.2 fusion.2
  2.1 1.2 fusion.3
  3.3 1.4 %fusion.1.onehot = bf16[2,256,32]{2,1,0:T(8,128)(2,1)} fusion(s32[2,32]{1,0:T(2,128)} %param.14, pred[2]{0:T(512)(128)(4,1)S(1)} %add_compare_fusion), kind=kLoop, calls=%fused_computation.5 | loop fusion | flops 49152 | bytes 33026 | tf_op jit(solution)/shard_map/convert_element_type | solution.py:265
  4.7 0.9 broadcast_in_dim_reshape.4.restore
  5.6 0.0 copy-start
  5.6 5.8 %add_convert_fusion.1.taps = bf16[192,2048]{1,0:T(8,128)(2,1)} fusion(f32[128,2048]{1,0:T(8,128)} %param.20, f32[2048]{0:T(1024)S(1)} %bitcast.32, f32[2048]{0:T(1024)S(1)} %bitcast.33, f32[2048]{0:T(1024)S(1)} %bitcast.28, f32[2048]{0:T(1024)S(1)} %bitcast.29, f32[2048]{0:T(1024)S(1)} %bitcast.30, f32[2048]{0:T(1024)S(1)} %bitcast.31, f32[2048]{0:T(1024)S(1)} %bitcast.27), kind=kLoop, calls=%fused_computation.2 | loop fusion | flops 5505024 | bytes 1892352 | tf_op jit(solution)/shard_map/convert_element_type | solution.py:239
  11.4 0.0 copy-done.1
  11.4 0.9 add_convert_fusion
  12.4 0.0 copy-done
  12.4 1.4 pad_maximum_fusion.own_ref
  13.8 114.5 %shard_map.118.projected = f32[768,2048]{1,0:T(8,128)} custom-call(bf16[4,112,2048]{2,1,0:T(8,128)(2,1)} %pad_maximum_fusion.own_ref, bf16[64,2048]{1,0:T(8,128)(2,1)} %bitcast.19, bf16[2,256,32]{2,1,0:T(8,128)(2,1)} %fusion.1.onehot, bf16[8192,2048]{1,0:T(8,128)(2,1)} %weight.1, bf16[512,256]{1,0:T(8,128)(2,1)} %constant.18.clone.forward, ...), custom_call_target="tpu_custom_call" | custom-call | tf_op jit(solution)/shard_map/pallas_call | solution.py:290
  128.3 12.5 %shard_map.119 = bf16[2,256,2048]{2,1,0:T(8,128)(2,1)} custom-call(bf16[256,2048]{1,0:T(8,128)(2,1)} %embed.1, bf16[2,32,2048]{2,1,0:T(8,128)(2,1)} %noise.1, bf16[2,256,32]{2,1,0:T(8,128)(2,1)} %fusion.1.onehot, s32[2,256,1]{2,1,0:T(8,128)} %broadcast_in_dim_reshape.4.restore, bf16[192,2048]{1,0:T(8,128)(2,1)} %add_convert_fusion.1.taps, ...), custom_call_target="tpu_custom_call" | custom-call | tf_op jit(solution)/shard_map/pallas_call | solution.py:321
  (1 shorter events, 0.0 us)
Async XLA Ops:
  0.0 11.4 %copy-start.1 = (f32[128,2048]{1,0:T(8,128)S(1)}, f32[128,2048]{1,0:T(8,128)}, u32[]{:S(2)}) copy-start(f32[128,2048]{1,0:T(8,128)} %param.17) | copy-start | bytes 3145732
  5.6 6.8 %copy-start = (bf16[256,2048]{1,0:T(8,128)(2,1)S(1)}, bf16[256,2048]{1,0:T(8,128)(2,1)}, u32[]{:S(2)}) copy-start(bf16[256,2048]{1,0:T(8,128)(2,1)} %embed.1) | copy-start | bytes 3145732

commit v4 on v2

--- a/solution.py
+++ b/solution.py
@@ -147,14 +147,14 @@
             from_core(k, m).wait_recv()
         from_chan(k)[1].wait_recv()
 
-    @pl.when((j == per - 2) & (k < chan_count - 1))
+    @pl.when((j == per - 3) & (k < chan_count - 1))
     def _():
         from_chan(k + 1)[0].wait_recv()
         for m in range(1, rows_x):
             to_row(k + 1, m).start()
         to_core(k + 1, 0).start()
 
-    @pl.when((j == per - 1) & (k < chan_count - 1))
+    @pl.when((j == per - 2) & (k < chan_count - 1))
     def _():
         for m in range(1, rows_x):
             from_row(k + 1, m).wait_recv()

time: 135 us -> 137 us (1.015)
  Pallas kernels: 121 us -> 123 us
    pallas_call x1, Pallas kernels: 108 us -> 111 us  [per_device(): pl.pallas_call(functools.partial(project_kernel, chan_count, run_devices,...]
where the time goes in v4:
time: 137 us
  Pallas kernels  123 us (90%)
  other arithmetic  9.56 us (7%)
  local copies, waits for them, and re-layouts  4.2 us (3%)
    pallas_call x1, Pallas kernels, per_device(): pl.pallas_call(functools.partial(project_kernel, chan_count, run_devices,...  111 us
    pallas_call x1, Pallas kernels, per_device(): pl.pallas_call(second_kernel, grid=(width // tile,), in_specs=[pl.BlockSp...  12.5 us
    convert_element_type x2, other arithmetic, combined_taps(): return total.astype(jnp.bfloat16)  6.74 us

profile of v4, /device:TPU:0, one launch (start us, length us, event | category | flops | bytes accessed | tf_op | source)
XLA Modules:
  0.0 137.0 jit_solution(3052619133989075545)
XLA Ops:
  0.0 0.0 copy-start.1
  0.0 0.8 broadcast_in_dim.2
  0.8 1.2 fusion.2
  2.1 1.2 fusion.3
  3.3 1.4 %fusion.1.onehot = bf16[2,256,32]{2,1,0:T(8,128)(2,1)} fusion(s32[2,32]{1,0:T(2,128)} %param.14, pred[2]{0:T(512)(128)(4,1)S(1)} %add_compare_fusion), kind=kLoop, calls=%fused_computation.5 | loop fusion | flops 49152 | bytes 33026 | tf_op jit(solution)/shard_map/convert_element_type | solution.py:250
  4.7 0.9 broadcast_in_dim_reshape.4.restore
  5.6 0.0 copy-start
  5.6 5.8 %add_convert_fusion.1.taps = bf16[192,2048]{1,0:T(8,128)(2,1)} fusion(f32[128,2048]{1,0:T(8,128)} %param.20, f32[2048]{0:T(1024)S(1)} %bitcast.32, f32[2048]{0:T(1024)S(1)} %bitcast.33, f32[2048]{0:T(1024)S(1)} %bitcast.28, f32[2048]{0:T(1024)S(1)} %bitcast.29, f32[2048]{0:T(1024)S(1)} %bitcast.30, f32[2048]{0:T(1024)S(1)} %bitcast.31, f32[2048]{0:T(1024)S(1)} %bitcast.27), kind=kLoop, calls=%fused_computation.2 | loop fusion | flops 5505024 | bytes 1892352 | tf_op jit(solution)/shard_map/convert_element_type | solution.py:224
  11.4 0.0 copy-done.1
  11.4 0.9 add_convert_fusion
  12.4 0.0 copy-done
  12.4 1.4 %pad_maximum_fusion.own_ref = bf16[4,112,2048]{2,1,0:T(8,128)(2,1)} fusion(bf16[4,48,2048]{2,1,0:T(8,128)(2,1)S(1)} %bitcast.18, bf16[4,64,2048]{2,1,0:T(8,128)(2,1)S(1)} %bitcast.17), kind=kLoop, calls=%fused_computation | loop fusion | flops 3670016 | bytes 3670016 | tf_op jit(solution)/shard_map/concatenate | solution.py:258
  13.8 110.7 %shard_map.118.projected = f32[768,2048]{1,0:T(8,128)} custom-call(bf16[4,112,2048]{2,1,0:T(8,128)(2,1)} %pad_maximum_fusion.own_ref, bf16[64,2048]{1,0:T(8,128)(2,1)} %bitcast.19, bf16[2,256,32]{2,1,0:T(8,128)(2,1)} %fusion.1.onehot, bf16[8192,2048]{1,0:T(8,128)(2,1)} %weight.1, bf16[512,256]{1,0:T(8,128)(2,1)} %constant.18.clone.forward, ...), custom_call_target="tpu_custom_call" | custom-call | tf_op jit(solution)/shard_map/pallas_call | solution.py:275
  124.5 12.5 %shard_map.119 = bf16[2,256,2048]{2,1,0:T(8,128)(2,1)} custom-call(bf16[256,2048]{1,0:T(8,128)(2,1)} %embed.1, bf16[2,32,2048]{2,1,0:T(8,128)(2,1)} %noise.1, bf16[2,256,32]{2,1,0:T(8,128)(2,1)} %fusion.1.onehot, s32[2,256,1]{2,1,0:T(8,128)} %broadcast_in_dim_reshape.4.restore, bf16[192,2048]{1,0:T(8,128)(2,1)} %add_convert_fusion.1.taps, ...), custom_call_target="tpu_custom_call" | custom-call | tf_op jit(solution)/shard_map/pallas_call | solution.py:306
  (1 shorter events, 0.0 us)
Async XLA Ops:
  0.0 11.4 %copy-start.1 = (f32[128,2048]{1,0:T(8,128)S(1)}, f32[128,2048]{1,0:T(8,128)}, u32[]{:S(2)}) copy-start(f32[128,2048]{1,0:T(8,128)} %param.17) | copy-start | bytes 3145732
  5.6 6.8 %copy-start = (bf16[256,2048]{1,0:T(8,128)(2,1)S(1)}, bf16[256,2048]{1,0:T(8,128)(2,1)}, u32[]{:S(2)}) copy-start(bf16[256,2048]{1,0:T(8,128)(2,1)} %embed.1) | copy-start | bytes 3145732
